TPU v7x, 32 devices: a whole 2x2x4 slice. The times are simulated.
32 devices in a mesh: gossip: 8 (over z, x), fsdp: 4 (over y, core).
Axes of the slice: x: 2, y: 2, z: 4, core: 2. Of those that a mesh axis runs over, the one named last changes fastest.
Arguments:
- inputs: bfloat16 [8, 2048, 2048], P('gossip', 'fsdp'), may hold values from -6 to 6
- out_grad: bfloat16 [8, 2048, 2048], P('gossip', 'fsdp'), may hold values from -6 to 6
- norm_gain: float32 [8, 2048], P('gossip'), may hold values from 0.5 to 1.5
- w_qkv: bfloat16 [8, 16, 2048, 384], P('gossip', 'fsdp'), may hold values from -64 to 64
- w_out: bfloat16 [8, 16, 128, 2048], P('gossip', 'fsdp'), may hold values from -6 to 6
- mom_qkv: bfloat16 [8, 16, 2048, 384], P('gossip', 'fsdp'), may hold values from -6 to 6
- mom_out: bfloat16 [8, 16, 128, 2048], P('gossip', 'fsdp'), may hold values from -6 to 6
- step_index: int32 [1], replicated, may hold values from 0 to 11
Outputs:
- new_qkv: bfloat16 [8, 16, 2048, 384], P('gossip', 'fsdp')
- new_out: bfloat16 [8, 16, 128, 2048], P('gossip', 'fsdp')
- new_mom_qkv: bfloat16 [8, 16, 2048, 384], P('gossip', 'fsdp')
- new_mom_out: bfloat16 [8, 16, 128, 2048], P('gossip', 'fsdp')
All inputs are finite; a program needn't handle non-finite values.
Results may differ from a plain program's by a relative error of at most 0.0085.
Values may be sent and summed in bfloat16 or wider, within the bound.
No kernel may reach another device: no remote copies, remote signals or barrier semaphores. Data moves between devices by JAX's collectives and lax.ppermute only.
A program may use at most 192 MiB of HBM per device.

v0:
```python
from functools import partial
import math

import jax
import jax.numpy as jnp
from jax import lax
from jax.experimental import pallas as pl
from jax.experimental.pallas import tpu as pltpu
from jax.sharding import PartitionSpec as P

HEADS = 16
LEVELS = 3

BETA = 0.9
RATE = 0.1
EPSILON = 1e-05

VMEM_LIMIT = 48 * 1024 * 1024
BLOCK = 256


def product(left, right, left_dim=1, right_dim=0):
    return lax.dot_general(
        left, right, (((left_dim,), (right_dim,)), ((), ())), preferred_element_type=jnp.float32
    )


def params():
    return pltpu.CompilerParams(vmem_limit_bytes=VMEM_LIMIT)


def shifted(value, by):
    size = lax.axis_size("gossip")
    return lax.ppermute(value, "gossip", [(i, (i + by) % size) for i in range(size)])


def rotary_tables(seq_len, head_dim):
    half = head_dim // 2
    frequency = jnp.exp(
        -math.log(10000.0) * 2.0 * jnp.arange(half, dtype=jnp.float32) / head_dim
    )
    angles = jnp.arange(seq_len).astype(jnp.float32)[:, None] * frequency[None, :]
    return jnp.cos(angles), jnp.sin(angles)


def project_kernel(scale, rows_ref, weight_ref, cos_ref, sin_ref, q_ref, k_ref, v_ref):
    rows = rows_ref[...]
    cosine, sine = cos_ref[...], sin_ref[...]
    width = cosine.shape[-1]
    for head in range(weight_ref.shape[0]):
        projected = product(rows, weight_ref[head]) * scale
        for which, out_ref in enumerate((q_ref, k_ref)):
            part = projected[:, which * width : (which + 1) * width]
            turned = part * cosine + pltpu.roll(part, width // 2, 1) * sine
            out_ref[head] = turned.astype(jnp.bfloat16)
        v_ref[head] = projected[:, 2 * width :].astype(jnp.bfloat16)


def project(rows, weights, cosine, sine):
    seq_len, width = rows.shape
    heads, _, three = weights.shape
    head_dim = three // 3
    block = min(BLOCK, seq_len)
    out = jax.ShapeDtypeStruct((heads, seq_len, head_dim), jnp.bfloat16)
    out_spec = pl.BlockSpec((heads, block, head_dim), lambda i: (0, i, 0))
    return pl.pallas_call(
        partial(project_kernel, 1.0 / math.sqrt(width)),
        grid=(seq_len // block,),
        in_specs=[
            pl.BlockSpec((block, width), lambda i: (i, 0)),
            pl.BlockSpec((heads, width, three), lambda i: (0, 0, 0)),
            pl.BlockSpec((block, head_dim), lambda i: (i, 0)),
            pl.BlockSpec((block, head_dim), lambda i: (i, 0)),
        ],
        out_specs=[out_spec] * 3,
        out_shape=[out] * 3,
        compiler_params=params(),
        cost_estimate=pl.CostEstimate(
            flops=2 * seq_len * width * heads * three,
            bytes_accessed=2 * (rows.size + weights.size + seq_len * heads * three),
            transcendentals=0,
        ),
        name="project",
    )(rows, weights, cosine, sine)


def cotangent_kernel(scale, rows_ref, weight_ref, out_ref):
    rows = rows_ref[...]
    for head in range(weight_ref.shape[0]):
        out_ref[head] = (product(rows, weight_ref[head], 1, 1) * scale).astype(jnp.bfloat16)


def cotangent(rows, weights, scale):
    seq_len, width = rows.shape
    heads, head_dim, _ = weights.shape
    block = min(2 * BLOCK, seq_len)
    return pl.pallas_call(
        partial(cotangent_kernel, scale),
        grid=(seq_len // block,),
        in_specs=[
            pl.BlockSpec((block, width), lambda i: (i, 0)),
            pl.BlockSpec((heads, head_dim, width), lambda i: (0, 0, 0)),
        ],
        out_specs=pl.BlockSpec((heads, block, head_dim), lambda i: (0, i, 0)),
        out_shape=jax.ShapeDtypeStruct((heads, seq_len, head_dim), jnp.bfloat16),
        compiler_params=params(),
        cost_estimate=pl.CostEstimate(
            flops=2 * seq_len * width * heads * head_dim,
            bytes_accessed=2 * (rows.size + weights.size + seq_len * heads * head_dim),
            transcendentals=0,
        ),
        name="cotangent",
    )(rows, weights)


def folded(values, combine):
    rows, columns = values.shape
    return combine(values.reshape(rows // 8, 8, columns), 0)


def attention_kernel(
    scale,
    proj_scale,
    q_ref,
    k_ref,
    v_ref,
    g_ref,
    cos_ref,
    sin_ref,
    grad_ref,
    att_ref,
    s_ref,
    p_ref,
    d_ref,
    kt_ref,
    vt_ref,
    gk_ref,
    gv_ref,
):
    step = pl.program_id(0)
    block = s_ref.shape[1]
    head_dim = q_ref.shape[-1]
    half = head_dim // 2

    here = pl.ds(pl.multiple_of(step * block, block), block)
    queries = q_ref[0, here, :]
    grads = g_ref[0, here, :]
    kt_ref[step] = k_ref[0, here, :].T
    vt_ref[step] = v_ref[0, here, :].T
    gk_ref[step] = jnp.zeros(gk_ref.shape[1:], jnp.float32)
    gv_ref[step] = jnp.zeros(gv_ref.shape[1:], jnp.float32)

    def rows(tile):
        return pl.ds(pl.multiple_of(tile * block, block), block)

    scores = product(k_ref[0, here, :], queries, 1, 1)
    key_pos = lax.broadcasted_iota(jnp.int32, scores.shape, 0)
    query_pos = lax.broadcasted_iota(jnp.int32, scores.shape, 1)
    scores = jnp.where(key_pos <= query_pos, scores, -jnp.inf)
    s_ref[step] = scores

    def score(tile, top):
        scores = product(k_ref[0, rows(tile), :], queries, 1, 1)
        s_ref[tile] = scores
        return jnp.maximum(top, folded(scores, jnp.max))

    top = lax.fori_loop(0, step, score, folded(scores, jnp.max))
    factor = scale * math.log2(math.e)
    top = jnp.max(top, 0, keepdims=True) * factor

    def weigh(tile, sums):
        total, inner = sums
        weights = jnp.exp2(s_ref[tile] * factor - top)
        grad_probs = product(v_ref[0, rows(tile), :], grads, 1, 1)
        p_ref[tile] = weights
        d_ref[tile] = grad_probs
        return total + folded(weights, jnp.sum), inner + folded(weights * grad_probs, jnp.sum)

    zeros = jnp.zeros((8, block), jnp.float32)
    total, inner = lax.fori_loop(0, step + 1, weigh, (zeros, zeros))
    inverse = 1.0 / jnp.sum(total, 0, keepdims=True)
    inner = jnp.sum(inner, 0, keepdims=True) * inverse

    def back(tile, sums):
        att, grad_q = sums
        probs = p_ref[tile] * inverse
        probs_b = probs.astype(jnp.bfloat16)
        grad_scores = (probs * (d_ref[tile] - inner)).astype(jnp.bfloat16)
        gv_ref[tile] += product(probs_b, grads)
        gk_ref[tile] += product(grad_scores, queries)
        return att + product(vt_ref[tile], probs_b), grad_q + product(kt_ref[tile], grad_scores)

    zeros = jnp.zeros((head_dim, block), jnp.float32)
    att, grad_q = lax.fori_loop(0, step + 1, back, (zeros, zeros))

    def unrotate(grad, where):
        cosine, sine = cos_ref[:, where], sin_ref[:, where]
        first, second = grad[:half], grad[half:]
        factor = scale * proj_scale
        return (
            ((first * cosine + second * sine) * factor).astype(jnp.bfloat16),
            ((second * cosine - first * sine) * factor).astype(jnp.bfloat16),
        )

    att_ref[:, here] = att.astype(jnp.bfloat16)
    first, second = unrotate(grad_q, here)
    grad_ref[:half, here] = first
    grad_ref[half:head_dim, here] = second

    @pl.when(step == pl.num_programs(0) - 1)
    def finish():
        def keys(tile, carry):
            where = rows(tile)
            first, second = unrotate(gk_ref[tile].T, where)
            grad_ref[head_dim : head_dim + half, where] = first
            grad_ref[head_dim + half : 2 * head_dim, where] = second
            values = gv_ref[tile].T * proj_scale
            grad_ref[2 * head_dim :, where] = values.astype(jnp.bfloat16)
            return carry

        lax.fori_loop(0, pl.num_programs(0), keys, 0)


def attention(head, queries, keys, values, grads, cosine_t, sine_t, width):
    _, seq_len, head_dim = queries.shape
    block = min(BLOCK, seq_len)
    tiles = seq_len // block
    of_head = pl.BlockSpec((1, seq_len, head_dim), lambda i: (head, 0, 0))
    whole = pl.BlockSpec((head_dim // 2, seq_len), lambda i: (0, 0))
    pairs = seq_len * (seq_len + block) // 2
    return pl.pallas_call(
        partial(attention_kernel, 1.0 / math.sqrt(head_dim), 1.0 / math.sqrt(width)),
        grid=(tiles,),
        in_specs=[of_head] * 4 + [whole] * 2,
        out_specs=[
            pl.BlockSpec((3 * head_dim, seq_len), lambda i: (0, 0)),
            pl.BlockSpec((head_dim, seq_len), lambda i: (0, 0)),
        ],
        out_shape=[
            jax.ShapeDtypeStruct((3 * head_dim, seq_len), jnp.bfloat16),
            jax.ShapeDtypeStruct((head_dim, seq_len), jnp.bfloat16),
        ],
        scratch_shapes=[pltpu.VMEM((tiles, block, block), jnp.float32)] * 3
        + [pltpu.VMEM((tiles, head_dim, block), jnp.bfloat16)] * 2
        + [pltpu.VMEM((tiles, block, head_dim), jnp.float32)] * 2,
        compiler_params=params(),
        cost_estimate=pl.CostEstimate(
            flops=12 * pairs * head_dim,
            bytes_accessed=2 * 8 * seq_len * head_dim,
            transcendentals=pairs,
        ),
        name="attention",
    )(queries, keys, values, grads, cosine_t, sine_t)


def momenta_kernel(
    scale, grad_ref, att_ref, normed_ref, rows_ref, mqkv_ref, mout_ref, moved_ref, moved_out_ref
):
    grad = product(grad_ref[...], normed_ref[...]).T.astype(jnp.bfloat16)
    moved = BETA * mqkv_ref[0].astype(jnp.float32) + grad.astype(jnp.float32)
    moved_ref[...] = moved.astype(jnp.bfloat16)
    grad = (product(att_ref[...], rows_ref[...]) * scale).astype(jnp.bfloat16)
    moved = BETA * mout_ref[0].astype(jnp.float32) + grad.astype(jnp.float32)
    moved_out_ref[...] = moved.astype(jnp.bfloat16)


def momenta(head, grad_proj, attended, normed, rows, mom_qkv, mom_out, scale):
    seq_len, width = normed.shape
    three, head_dim = grad_proj.shape[0], attended.shape[0]
    block = min(BLOCK, width)
    return pl.pallas_call(
        partial(momenta_kernel, scale),
        grid=(width // block,),
        in_specs=[
            pl.BlockSpec((three, seq_len), lambda i: (0, 0)),
            pl.BlockSpec((head_dim, seq_len), lambda i: (0, 0)),
            pl.BlockSpec((seq_len, block), lambda i: (0, i)),
            pl.BlockSpec((seq_len, block), lambda i: (0, i)),
            pl.BlockSpec((1, block, three), lambda i: (head, i, 0)),
            pl.BlockSpec((1, head_dim, block), lambda i: (head, 0, i)),
        ],
        out_specs=[
            pl.BlockSpec((block, three), lambda i: (i, 0)),
            pl.BlockSpec((head_dim, block), lambda i: (0, i)),
        ],
        out_shape=[
            jax.ShapeDtypeStruct((width, three), jnp.bfloat16),
            jax.ShapeDtypeStruct((head_dim, width), jnp.bfloat16),
        ],
        compiler_params=params(),
        cost_estimate=pl.CostEstimate(
            flops=2 * seq_len * width * (three + head_dim),
            bytes_accessed=2 * (2 * seq_len * width + 3 * width * (three + head_dim)),
            transcendentals=0,
        ),
        name="momenta",
    )(grad_proj, attended, normed, rows, mom_qkv, mom_out)


def average_kernel(rate_ref, *refs):
    rate = rate_ref[0, 0]
    outs = refs[-4:]

    def halfway(own, other):
        return ((own.astype(jnp.float32) + other.astype(jnp.float32)) * 0.5).astype(jnp.bfloat16)

    def moved(weight, moment):
        new = weight.astype(jnp.float32) - rate * moment.astype(jnp.float32)
        return new.astype(jnp.bfloat16)

    for part in range(2):
        weight, other_weight, moment, other_moment = (r for r in refs[4 * part : 4 * part + 4])
        own_m, other_m = moment[...], other_moment[...]
        own_w = moved(weight[0], own_m)
        other_w = moved(other_weight[0], other_m)
        outs[part][0] = halfway(own_w, other_w)
        outs[2 + part][0] = halfway(own_m, other_m)


def average(head, rate, own, other, moments, other_moments, previous):
    heads = own[0].shape[0]
    steps = 4
    in_specs = [pl.BlockSpec(memory_space=pltpu.SMEM)]
    args = [rate]
    out_specs, out_shape = [], []
    for part in range(2):
        _, high, wide = own[part].shape
        stacked = pl.BlockSpec((1, high // steps, wide), lambda i: (head, i, 0))
        single = pl.BlockSpec((high // steps, wide), lambda i: (i, 0))
        in_specs += [stacked, stacked, single, single]
        args += [own[part], other[part], moments[part], other_moments[part]]
        out_specs.append(stacked)
        out_shape.append(jax.ShapeDtypeStruct((heads, high, wide), jnp.bfloat16))
    aliases = {}
    if previous is not None:
        aliases = {len(args) + i: i for i in range(4)}
        args += list(previous)
        in_specs += [pl.BlockSpec(memory_space=pl.ANY)] * 4
    return pl.pallas_call(
        average_kernel,
        grid=(steps,),
        in_specs=in_specs,
        out_specs=out_specs * 2,
        out_shape=out_shape * 2,
        input_output_aliases=aliases,
        compiler_params=params(),
        cost_estimate=pl.CostEstimate(
            flops=10 * sum(m.size for m in moments),
            bytes_accessed=12 * sum(m.size for m in moments),
            transcendentals=0,
        ),
        name="average",
    )(*args)


def update(by, inputs, out_grad, norm_gain, w_qkv, w_out, mom_qkv, mom_out, rate):
    own = (w_qkv, w_out)
    other = tuple(shifted(w, by) for w in own)

    rows_f = inputs.astype(jnp.float32)
    stats = lax.rsqrt(jnp.mean(rows_f * rows_f, -1, keepdims=True) + EPSILON)
    normed = (rows_f * stats * norm_gain[None, :]).astype(jnp.bfloat16)
    normed = lax.all_gather(normed, "fsdp", axis=0, tiled=True)
    rows = lax.all_gather(out_grad, "fsdp", axis=0, tiled=True)

    seq_len, width = normed.shape
    heads, head_dim, _ = w_out.shape
    out_scale = 1.0 / math.sqrt(HEADS * head_dim)
    cosine, sine = rotary_tables(seq_len, head_dim)
    queries, keys, values = project(
        normed,
        w_qkv,
        jnp.concatenate([cosine, cosine], -1),
        jnp.concatenate([-sine, sine], -1),
    )
    grads = cotangent(rows, w_out, out_scale)
    moments, other_moments = [], []
    for head in range(heads):
        grad_proj, attended = attention(
            head, queries, keys, values, grads, cosine.T, sine.T, width
        )
        moved = momenta(head, grad_proj, attended, normed, rows, mom_qkv, mom_out, out_scale)
        moments.append(moved)
        other_moments.append([shifted(m, by) for m in moved])
    results = None
    for head in range(heads):
        results = average(head, rate, own, other, moments[head], other_moments[head], results)
    return tuple(results)


def per_device(inputs, out_grad, norm_gain, w_qkv, w_out, mom_qkv, mom_out, step_index):
    rate = RATE * (step_index[0].astype(jnp.float32) + 1.0) / (4.0 * LEVELS)
    exponent = jnp.remainder(step_index[0], LEVELS)
    results = lax.switch(
        exponent,
        [partial(update, 1 << level) for level in range(LEVELS)],
        inputs[0],
        out_grad[0],
        norm_gain[0],
        w_qkv[0],
        w_out[0],
        mom_qkv[0],
        mom_out[0],
        rate.reshape(1, 1),
    )
    return tuple(r[None] for r in results)


def solution(mesh):
    return jax.shard_map(
        per_device,
        mesh=mesh,
        in_specs=(
            P("gossip", "fsdp", None),
            P("gossip", "fsdp", None),
            P("gossip", None),
            P("gossip", "fsdp", None, None),
            P("gossip", "fsdp", None, None),
            P("gossip", "fsdp", None, None),
            P("gossip", "fsdp", None, None),
            P(),
        ),
        out_specs=(
            P("gossip", "fsdp", None, None),
            P("gossip", "fsdp", None, None),
            P("gossip", "fsdp", None, None),
            P("gossip", "fsdp", None, None),
        ),
        check_vma=False,
    )
```

profile of v0, /device:TPU:0, one launch (start us, length us, event | category | flops | bytes accessed | tf_op | source)
XLA Modules:
  0.0 455.9 jit_solution(2858665363720567125)
XLA Ops:
  7.8 434.8 %conditional.1 = ((bf16[4,2048,384]{2,1,0:T(8,128)(2,1)}, bf16[4,128,2048]{2,1,0:T(8,128)(2,1)}, bf16[4,2048,384]{2,1,0:T(8,128)(2,1)}, bf16[4,128,2048]{2,1,0:T...) conditional(s32[]{:T(128)} %clamp.3, (s32[]{:T(128)}, ...), branch_computations={%region_0.2_spmd, %region_2.4_spmd, %region_4.6_spmd} | conditional | flops 48905457664 | bytes 522266688 | solution.py:394
  13.9 0.0 copy-start.70
  14.0 0.0 all-gather.16.cloned.1.call-start
  14.0 0.0 copy-start.77
  14.0 0.7 all-gather.16.cloned.1.call-update
  14.7 0.0 all-gather.14.cloned.1.call-start
  14.7 0.8 copy-done.70
  15.5 0.5 fusion.4
  16.0 1.9 fusion.6
  17.9 0.0 all-gather.14.cloned.1.call-update
  17.9 3.1 collective-permute-start.10
  21.0 1.6 collective-permute-start.12
  22.6 3.7 fusion.7
  26.3 0.6 pad_maximum_fusion.2
  26.9 1.9 multiply_sine_fusion.3
  28.9 48.5 %all-gather.16.cloned.1.call-done = bf16[1,2048,2048]{2,1,0:T(8,128)(2,1)} async-done(((bf16[1,512,2048]{2,1,0:T(8,128)(2,1)}), bf16[1,2048,2048]{2,1,0:T(8,128)(2,1)}) %all-gather.16.cloned.1.call-update) | async-done | bytes 8388624 | tf_op jit(solution)/shard_map/cond/branch_1_fun/all_gather | solution.py:364
  77.4 11.8 %cotangent.4.g_ref = bf16[4,2048,128]{2,1,0:T(8,128)(2,1)S(1)} custom-call(bf16[2048,2048]{1,0:T(8,128)(2,1)} %bitcast.92, bf16[4,128,2048]{2,1,0:T(8,128)(2,1)} %bitcast.15.weight_ref.refs_4_), custom_call_target="tpu_custom_call" | custom-call | flops 4294967296 | bytes 12582912 | tf_op jit(solution)/shard_map/cond/branch_1_fun/cotangent/pallas_call | solution.py:97
  89.2 0.0 copy-start.49
  89.2 1.3 copy-done.49
  90.5 47.3 %all-gather.14.cloned.1.call-done.rows_ref.normed_ref = bf16[2048,2048]{1,0:T(8,128)(2,1)} async-done(((bf16[512,2048]{1,0:T(8,128)(2,1)}), bf16[2048,2048]{1,0:T(8,128)(2,1)}) %all-gather.14.cloned.1.call-update) | async-done | bytes 8388624 | tf_op jit(solution)/shard_map/cond/branch_1_fun/all_gather | solution.py:363
  137.8 23.4 %project.4 = (bf16[4,2048,128]{2,1,0:T(8,128)(2,1)S(1)}, bf16[4,2048,128]{2,1,0:T(8,128)(2,1)}, bf16[4,2048,128]{2,1,0:T(8,128)(2,1)}) custom-call(bf16[2048,2048]{1,0:T(8,128)(2,1)} %all-gather.14.cloned.1.call-done.rows_ref.normed_ref, bf16[4,2048,384]{2,1,0:T(8,128)(2,1)} %bitcast.46, f32[2048,128]{1,0:T(8,128)S(1)} %get-tuple-element.251.cos_ref, ...), custom_call_target="tpu_custom_call" | custom-call | flops 12884901888 | bytes 20971520 | tf_op jit(solution)/shard_map/cond/branch_1_fun/project/pallas_call | solution.py:66
  161.3 0.0 copy-start.65
  161.3 28.4 %attention.19 = (bf16[384,2048]{1,0:T(8,128)(2,1)S(1)}, bf16[128,2048]{1,0:T(8,128)(2,1)S(1)}) custom-call(bf16[4,2048,128]{2,1,0:T(8,128)(2,1)S(1)} %get-tuple-element.147.q_ref, bf16[4,2048,128]{2,1,0:T(8,128)(2,1)} %get-tuple-element.148.k_ref, bf16[4,2048,128]{2,1,0:T(8,128)(2,1)} %get-tuple-element.149.v_ref, bf16[4,2048,128]{2,1,0:T(8,128)(2,1)} %copy-done.49, ...), custom_call_target="tpu_custom_call" | custom-call | flops 3623878656 | bytes 4194304 | tf_op jit(solution)/shard_map/cond/branch_1_fun/attention/pallas_call | solution.py:231
  189.8 10.7 %momenta.19 = (bf16[2048,384]{1,0:T(8,128)(2,1)S(1)}, bf16[128,2048]{1,0:T(8,128)(2,1)S(1)}) custom-call(bf16[384,2048]{1,0:T(8,128)(2,1)S(1)} %get-tuple-element.166.grad_ref, bf16[128,2048]{1,0:T(8,128)(2,1)S(1)} %get-tuple-element.167.att_ref, bf16[2048,2048]{1,0:T(8,128)(2,1)} %all-gather.14.cloned.1.call-done.rows_ref.normed_ref, ...), custom_call_target="tpu_custom_call" | custom-call | flops 4294967296 | bytes 23068672 | tf_op jit(solution)/shard_map/cond/branch_1_fun/momenta/pallas_call | solution.py:271
  200.5 1.5 collective-permute-start.19
  202.0 1.5 collective-permute-start.18
  203.5 27.6 %attention.18 = (bf16[384,2048]{1,0:T(8,128)(2,1)S(1)}, bf16[128,2048]{1,0:T(8,128)(2,1)S(1)}) custom-call(bf16[4,2048,128]{2,1,0:T(8,128)(2,1)S(1)} %get-tuple-element.147.q_ref, bf16[4,2048,128]{2,1,0:T(8,128)(2,1)} %get-tuple-element.148.k_ref, bf16[4,2048,128]{2,1,0:T(8,128)(2,1)} %get-tuple-element.149.v_ref, bf16[4,2048,128]{2,1,0:T(8,128)(2,1)} %copy-done.49, ...), custom_call_target="tpu_custom_call" | custom-call | flops 3623878656 | bytes 4194304 | tf_op jit(solution)/shard_map/cond/branch_1_fun/attention/pallas_call | solution.py:231
  231.2 0.0 copy-start.54
  231.2 11.1 %momenta.18 = (bf16[2048,384]{1,0:T(8,128)(2,1)S(1)}, bf16[128,2048]{1,0:T(8,128)(2,1)S(1)}) custom-call(bf16[384,2048]{1,0:T(8,128)(2,1)S(1)} %get-tuple-element.162.grad_ref, bf16[128,2048]{1,0:T(8,128)(2,1)S(1)} %get-tuple-element.163.att_ref, bf16[2048,2048]{1,0:T(8,128)(2,1)} %all-gather.14.cloned.1.call-done.rows_ref.normed_ref, ...), custom_call_target="tpu_custom_call" | custom-call | flops 4294967296 | bytes 23068672 | tf_op jit(solution)/shard_map/cond/branch_1_fun/momenta/pallas_call | solution.py:271
  242.3 1.5 collective-permute-start.16
  243.8 27.6 %attention.17 = (bf16[384,2048]{1,0:T(8,128)(2,1)S(1)}, bf16[128,2048]{1,0:T(8,128)(2,1)S(1)}) custom-call(bf16[4,2048,128]{2,1,0:T(8,128)(2,1)S(1)} %copy-done.54, bf16[4,2048,128]{2,1,0:T(8,128)(2,1)} %get-tuple-element.148.k_ref, bf16[4,2048,128]{2,1,0:T(8,128)(2,1)} %get-tuple-element.149.v_ref, bf16[4,2048,128]{2,1,0:T(8,128)(2,1)} %copy-done.49, ...), custom_call_target="tpu_custom_call" | custom-call | flops 3623878656 | bytes 4194304 | tf_op jit(solution)/shard_map/cond/branch_1_fun/attention/pallas_call | solution.py:231
  271.5 27.8 %attention.16 = (bf16[384,2048]{1,0:T(8,128)(2,1)S(1)}, bf16[128,2048]{1,0:T(8,128)(2,1)S(1)}) custom-call(bf16[4,2048,128]{2,1,0:T(8,128)(2,1)S(1)} %copy-done.54, bf16[4,2048,128]{2,1,0:T(8,128)(2,1)} %get-tuple-element.148.k_ref, bf16[4,2048,128]{2,1,0:T(8,128)(2,1)} %get-tuple-element.149.v_ref, bf16[4,2048,128]{2,1,0:T(8,128)(2,1)} %copy-done.49, ...), custom_call_target="tpu_custom_call" | custom-call | flops 3623878656 | bytes 4194304 | tf_op jit(solution)/shard_map/cond/branch_1_fun/attention/pallas_call | solution.py:231
  299.3 11.8 %momenta.17 = (bf16[2048,384]{1,0:T(8,128)(2,1)}, bf16[128,2048]{1,0:T(8,128)(2,1)}) custom-call(bf16[384,2048]{1,0:T(8,128)(2,1)S(1)} %get-tuple-element.158.grad_ref, bf16[128,2048]{1,0:T(8,128)(2,1)S(1)} %get-tuple-element.159.att_ref, bf16[2048,2048]{1,0:T(8,128)(2,1)} %all-gather.14.cloned.1.call-done.rows_ref.normed_ref, bf16[2048,2048]{1,0:T(8,128)(2,1)} %bitcast.95, ...), custom_call_target="tpu_custom_call" | custom-call | flops 4294967296 | bytes 23068672 | tf_op jit(solution)/shard_map/cond/branch_1_fun/momenta/pallas_call | solution.py:271
  311.1 0.6 collective-permute-start.14
  311.7 11.5 %momenta.16 = (bf16[2048,384]{1,0:T(8,128)(2,1)S(1)}, bf16[128,2048]{1,0:T(8,128)(2,1)}) custom-call(bf16[384,2048]{1,0:T(8,128)(2,1)S(1)} %get-tuple-element.152.grad_ref, bf16[128,2048]{1,0:T(8,128)(2,1)S(1)} %get-tuple-element.153.att_ref, bf16[2048,2048]{1,0:T(8,128)(2,1)} %all-gather.14.cloned.1.call-done.rows_ref.normed_ref, ...), custom_call_target="tpu_custom_call" | custom-call | flops 4294967296 | bytes 23068672 | tf_op jit(solution)/shard_map/cond/branch_1_fun/momenta/pallas_call | solution.py:271
  323.2 1.5 collective-permute-start.11
  324.6 0.8 copy-done.32
  325.4 1.4 collective-permute-start.17
  326.9 67.0 %collective-permute-done.17.refs_7_ = bf16[128,2048]{1,0:T(8,128)(2,1)S(1)} collective-permute-done((bf16[128,2048]{1,0:T(8,128)(2,1)S(1)}, bf16[128,2048]{1,0:T(8,128)(2,1)S(1)}, u32[]{:S(2)}, u32[]{:S(2)}) %collective-permute-start.17) | collective-permute-done | bytes 524320 | tf_op jit(solution)/shard_map/cond/branch_1_fun/ppermute | solution.py:34
  393.9 0.8 copy-done.20
  394.7 1.1 copy-done.8
  395.8 0.2 collective-permute-start.13
  396.6 1.4 copy-done.3
  398.0 1.4 copy-done.9
  399.5 1.0 copy-done.27
  400.5 1.0 copy-done.33
  401.5 4.9 %average.16 = (bf16[4,2048,384]{2,1,0:T(8,128)(2,1)S(1)}, bf16[4,128,2048]{2,1,0:T(8,128)(2,1)}, bf16[4,2048,384]{2,1,0:T(8,128)(2,1)}, bf16[4,128,2048]{2,1,0:T(8,128)(2,1)}) custom-call(f32[1,1]{1,0:T(1,128)} %bitcast.9.rate_ref, bf16[4,2048,384]{2,1,0:T(8,128)(2,1)} %bitcast.47, bf16[4,2048,384]{2,1,0:T(8,128)(2,1)} %collective-permute-done.10.refs_1_, ...), custom_call_target="tpu_custom_call" | custom-call | flops 10485760 | bytes 12582912 | tf_op jit(solution)/shard_map/cond/branch_1_fun/average/pallas_call | solution.py:339
  406.5 5.1 %average.17 = (bf16[4,2048,384]{2,1,0:T(8,128)(2,1)S(1)}, bf16[4,128,2048]{2,1,0:T(8,128)(2,1)}, bf16[4,2048,384]{2,1,0:T(8,128)(2,1)}, bf16[4,128,2048]{2,1,0:T(8,128)(2,1)}) custom-call(f32[1,1]{1,0:T(1,128)} %bitcast.9.rate_ref, bf16[4,2048,384]{2,1,0:T(8,128)(2,1)} %bitcast.48, ...), custom_call_target="tpu_custom_call", output_to_operand_aliasing={{0}: (9, {}), {1}: (10, {}), {2}: (11, {}), {3}: (12, {})} | custom-call | flops 10485760 | bytes 12582912 | tf_op jit(solution)/shard_map/cond/branch_1_fun/average/pallas_call | solution.py:339
  411.6 0.1 collective-permute-done.15.refs_7_
  411.6 5.6 %average.18 = (bf16[4,2048,384]{2,1,0:T(8,128)(2,1)S(1)}, bf16[4,128,2048]{2,1,0:T(8,128)(2,1)}, bf16[4,2048,384]{2,1,0:T(8,128)(2,1)}, bf16[4,128,2048]{2,1,0:T(8,128)(2,1)}) custom-call(f32[1,1]{1,0:T(1,128)} %bitcast.9.rate_ref, bf16[4,2048,384]{2,1,0:T(8,128)(2,1)} %bitcast.49, ...), custom_call_target="tpu_custom_call", output_to_operand_aliasing={{0}: (9, {}), {1}: (10, {}), {2}: (11, {}), {3}: (12, {})} | custom-call | flops 10485760 | bytes 12582912 | tf_op jit(solution)/shard_map/cond/branch_1_fun/average/pallas_call | solution.py:339
  417.2 3.2 collective-permute-done.13.refs_7_
  420.4 5.3 %average.19 = (bf16[4,2048,384]{2,1,0:T(8,128)(2,1)S(1)}, bf16[4,128,2048]{2,1,0:T(8,128)(2,1)}, bf16[4,2048,384]{2,1,0:T(8,128)(2,1)}, bf16[4,128,2048]{2,1,0:T(8,128)(2,1)}) custom-call(f32[1,1]{1,0:T(1,128)} %bitcast.9.rate_ref, bf16[4,2048,384]{2,1,0:T(8,128)(2,1)} %bitcast.50, ...), custom_call_target="tpu_custom_call", output_to_operand_aliasing={{0}: (9, {}), {1}: (10, {}), {2}: (11, {}), {3}: (12, {})} | custom-call | flops 10485760 | bytes 12582912 | tf_op jit(solution)/shard_map/cond/branch_1_fun/average/pallas_call | solution.py:339
  425.6 0.6 copy.125
  426.3 2.2 copy-done.58
  428.5 0.3 copy-done.61
  428.8 0.1 copy.126
  428.9 2.8 copy.127
  431.7 1.6 copy.128
  442.6 0.0 copy-start.72
  442.6 0.0 copy-start.73
  442.6 2.7 copy-done.72
  445.3 2.1 copy-done.73
  447.4 0.5 copy-done.74
  447.9 0.6 copy-done.75
  (52 shorter events, 0.1 us)
Async XLA Ops:
  13.9 1.6 copy-start.70
  14.0 63.4 %all-gather.16.cloned.1.call-start = ((), (), s32[]{:S(2)}) async-start(), calls=%async_computation.3 | async-start | bytes 10485760 | tf_op jit(solution)/shard_map/cond/branch_1_fun/all_gather | solution.py:364
  14.0 2.0 copy-start.77
  14.7 123.1 %all-gather.14.cloned.1.call-start = ((), (), s32[]{:S(2)}) async-start(), calls=%async_computation.2 | async-start | bytes 10485760 | tf_op jit(solution)/shard_map/cond/branch_1_fun/all_gather | solution.py:363
  17.9 305.2 %collective-permute-start.10 = (bf16[4,2048,384]{2,1,0:T(8,128)(2,1)}, bf16[4,2048,384]{2,1,0:T(8,128)(2,1)}, u32[]{:S(2)}, u32[]{:S(2)}) collective-permute-start(bf16[4,2048,384]{2,1,0:T(8,128)(2,1)} %bitcast.45), channel_id=1, source_target_pairs={{0,8},{4,12},{8,16},{12,20},{16,24},{20,28},{24,0},{28,4},{1,9},{5... | collective-permute-start | bytes 18874376 | tf_op jit(solution)/shard_map/cond/branch_1_fun/ppermute | solution.py:34
  21.0 290.1 %collective-permute-start.12 = (bf16[4,128,2048]{2,1,0:T(8,128)(2,1)}, bf16[4,128,2048]{2,1,0:T(8,128)(2,1)}, u32[]{:S(2)}, u32[]{:S(2)}) collective-permute-start(bf16[4,128,2048]{2,1,0:T(8,128)(2,1)} %bitcast.15.weight_ref.refs_4_), channel_id=1, source_target_pairs={{0,8},{4,12},{8,16},{12,20},{16,24},{20,28},{24,0},{28,4},{1,9},{5... | collective-permute-start | bytes 6291464 | tf_op jit(solution)/shard_map/cond/branch_1_fun/ppermute | solution.py:34
  28.8 174.7 %copy-start.40 = (f32[64,2048]{1,0:T(8,128)}, f32[64,2048]{1,0:T(8,128)S(1)}, u32[]{:S(2)}) copy-start(f32[64,2048]{1,0:T(8,128)S(1)} %get-tuple-element.246.sin_ref) | copy-start | bytes 1572868 | tf_op jit(solution)/shard_map/cond
  28.8 174.7 %copy-start.42 = (f32[64,2048]{1,0:T(8,128)}, f32[64,2048]{1,0:T(8,128)S(1)}, u32[]{:S(2)}) copy-start(f32[64,2048]{1,0:T(8,128)S(1)} %get-tuple-element.247.cos_ref) | copy-start | bytes 1572868 | tf_op jit(solution)/shard_map/cond
  89.2 1.3 copy-start.49
  161.3 42.3 %copy-start.53 = (bf16[4,2048,128]{2,1,0:T(8,128)(2,1)}, bf16[4,2048,128]{2,1,0:T(8,128)(2,1)S(1)}, u32[]{:S(2)}) copy-start(bf16[4,2048,128]{2,1,0:T(8,128)(2,1)S(1)} %get-tuple-element.147.q_ref) | copy-start | bytes 6291460 | tf_op jit(solution)/shard_map/cond
  161.3 28.4 %slice-start.2 = ((s8[6291456]{0:T(1024)(128)(4,1)}), s8[4194304]{0:T(1024)(128)(4,1)S(1)}, s32[]{:S(2)}) async-start(s8[6291456]{0:T(1024)(128)(4,1)} %bitcast.66), calls=%async_computation.8 | async-start | bytes 8388608 | tf_op jit(solution)/shard_map/cond
  161.3 28.5 %slice-start.3 = ((s8[6291456]{0:T(1024)(128)(4,1)}), s8[2097152]{0:T(1024)(128)(4,1)S(1)}, s32[]{:S(2)}) async-start(s8[6291456]{0:T(1024)(128)(4,1)} %bitcast.66), calls=%async_computation.9 | async-start | bytes 4194304 | tf_op jit(solution)/shard_map/cond
  161.3 28.5 %copy-start.65 = (bf16[1,4,128,2048]{3,2,1,0:T(8,128)(2,1)S(1)}, bf16[1,4,128,2048]{3,2,1,0:T(8,128)(2,1)}, u32[]{:S(2)}) copy-start(bf16[1,4,128,2048]{3,2,1,0:T(8,128)(2,1)} %get-tuple-element.155) | copy-start | bytes 6291460 | tf_op jit(solution)/shard_map/cond
  200.5 30.7 %copy-start.2 = (bf16[2048,384]{1,0:T(8,128)(2,1)}, bf16[2048,384]{1,0:T(8,128)(2,1)S(1)}, u32[]{:S(2)}) copy-start(bf16[2048,384]{1,0:T(8,128)(2,1)S(1)} %get-tuple-element.168.refs_2_) | copy-start | bytes 4718596 | tf_op jit(solution)/shard_map/cond
  200.5 30.7 %copy-start.26 = (bf16[128,2048]{1,0:T(8,128)(2,1)}, bf16[128,2048]{1,0:T(8,128)(2,1)S(1)}, u32[]{:S(2)}) copy-start(bf16[128,2048]{1,0:T(8,128)(2,1)S(1)} %get-tuple-element.169.refs_6_) | copy-start | bytes 1572868 | tf_op jit(solution)/shard_map/cond
  200.5 124.1 %collective-permute-start.19 = (bf16[128,2048]{1,0:T(8,128)(2,1)S(1)}, bf16[128,2048]{1,0:T(8,128)(2,1)S(1)}, u32[]{:S(2)}, u32[]{:S(2)}) collective-permute-start(bf16[128,2048]{1,0:T(8,128)(2,1)S(1)} %get-tuple-element.169.refs_6_), channel_id=1, source_target_pairs={{0,8},{4,12},{8,16},{12,20},{16,24},{20,28},{24,0},{28,4},{1,9},{5... | collective-permute-start | bytes 1572872 | tf_op jit(solution)/shard_map/cond/branch_1_fun/ppermute | solution.py:34
  202.0 192.6 %collective-permute-start.18 = (bf16[2048,384]{1,0:T(8,128)(2,1)S(1)}, bf16[2048,384]{1,0:T(8,128)(2,1)S(1)}, u32[]{:S(2)}, u32[]{:S(2)}) collective-permute-start(bf16[2048,384]{1,0:T(8,128)(2,1)S(1)} %get-tuple-element.168.refs_2_), channel_id=1, source_target_pairs={{0,8},{4,12},{8,16},{12,20},{16,24},{20,28},{24,0},{28,4},{1,9},{5... | collective-permute-start | bytes 4718600 | tf_op jit(solution)/shard_map/cond/branch_1_fun/ppermute | solution.py:34
  231.2 12.7 %copy-start.41 = (f32[64,2048]{1,0:T(8,128)S(1)}, f32[64,2048]{1,0:T(8,128)}, u32[]{:S(2)}) copy-start(f32[64,2048]{1,0:T(8,128)} %copy-done.40) | copy-start | bytes 1572868 | tf_op jit(solution)/shard_map/cond
  231.2 12.7 %copy-start.43 = (f32[64,2048]{1,0:T(8,128)S(1)}, f32[64,2048]{1,0:T(8,128)}, u32[]{:S(2)}) copy-start(f32[64,2048]{1,0:T(8,128)} %copy-done.42) | copy-start | bytes 1572868 | tf_op jit(solution)/shard_map/cond
  231.2 12.7 %copy-start.54 = (bf16[4,2048,128]{2,1,0:T(8,128)(2,1)S(1)}, bf16[4,2048,128]{2,1,0:T(8,128)(2,1)}, u32[]{:S(2)}) copy-start(bf16[4,2048,128]{2,1,0:T(8,128)(2,1)} %copy-done.53) | copy-start | bytes 6291460 | tf_op jit(solution)/shard_map/cond
  242.3 83.1 %copy-start.14 = (bf16[128,2048]{1,0:T(8,128)(2,1)}, bf16[128,2048]{1,0:T(8,128)(2,1)S(1)}, u32[]{:S(2)}) copy-start(bf16[128,2048]{1,0:T(8,128)(2,1)S(1)} %get-tuple-element.165.refs_6_) | copy-start | bytes 1572868 | tf_op jit(solution)/shard_map/cond
  242.3 164.1 %collective-permute-start.16 = (bf16[2048,384]{1,0:T(8,128)(2,1)S(1)}, bf16[2048,384]{1,0:T(8,128)(2,1)}, u32[]{:S(2)}, u32[]{:S(2)}) collective-permute-start(bf16[2048,384]{1,0:T(8,128)(2,1)S(1)} %get-tuple-element.164.refs_2_), channel_id=1, source_target_pairs={{0,8},{4,12},{8,16},{12,20},{16,24},{20,28},{24,0},{28,4},{1,9},{5... | collective-permute-start | bytes 4718600 | tf_op jit(solution)/shard_map/cond/branch_1_fun/ppermute | solution.py:34
  271.5 27.8 %copy-start.66 = (bf16[1,4,128,2048]{3,2,1,0:T(8,128)(2,1)S(1)}, bf16[1,4,128,2048]{3,2,1,0:T(8,128)(2,1)}, u32[]{:S(2)}) copy-start(bf16[1,4,128,2048]{3,2,1,0:T(8,128)(2,1)} %get-tuple-element.155) | copy-start | bytes 6291460 | tf_op jit(solution)/shard_map/cond
  311.1 100.5 %collective-permute-start.14 = (bf16[2048,384]{1,0:T(8,128)(2,1)}, bf16[2048,384]{1,0:T(8,128)(2,1)}, u32[]{:S(2)}, u32[]{:S(2)}) collective-permute-start(bf16[2048,384]{1,0:T(8,128)(2,1)} %get-tuple-element.160.refs_2_), channel_id=1, source_target_pairs={{0,8},{4,12},{8,16},{12,20},{16,24},{20,28},{24,0},{28,4},{1,9},{5... | collective-permute-start | bytes 4718600 | tf_op jit(solution)/shard_map/cond/branch_1_fun/ppermute | solution.py:34
  323.2 97.2 %collective-permute-start.11 = (bf16[2048,384]{1,0:T(8,128)(2,1)S(1)}, bf16[2048,384]{1,0:T(8,128)(2,1)}, u32[]{:S(2)}, u32[]{:S(2)}) collective-permute-start(bf16[2048,384]{1,0:T(8,128)(2,1)S(1)} %get-tuple-element.156.refs_2_), channel_id=1, source_target_pairs={{0,8},{4,12},{8,16},{12,20},{16,24},{20,28},{24,0},{28,4},{1,9},{5... | collective-permute-start | bytes 4718600 | tf_op jit(solution)/shard_map/cond/branch_1_fun/ppermute | solution.py:34
  324.6 0.8 copy-start.32
  325.4 68.4 %collective-permute-start.17 = (bf16[128,2048]{1,0:T(8,128)(2,1)S(1)}, bf16[128,2048]{1,0:T(8,128)(2,1)S(1)}, u32[]{:S(2)}, u32[]{:S(2)}) collective-permute-start(bf16[128,2048]{1,0:T(8,128)(2,1)S(1)} %get-tuple-element.165.refs_6_), channel_id=1, source_target_pairs={{0,8},{4,12},{8,16},{12,20},{16,24},{20,28},{24,0},{28,4},{1,9},{5... | collective-permute-start | bytes 1572872 | tf_op jit(solution)/shard_map/cond/branch_1_fun/ppermute | solution.py:34
  393.9 0.8 copy-start.20
  394.7 17.0 %collective-permute-start.15 = (bf16[128,2048]{1,0:T(8,128)(2,1)}, bf16[128,2048]{1,0:T(8,128)(2,1)}, u32[]{:S(2)}, u32[]{:S(2)}) collective-permute-start(bf16[128,2048]{1,0:T(8,128)(2,1)} %get-tuple-element.161.refs_6_), channel_id=1, source_target_pairs={{0,8},{4,12},{8,16},{12,20},{16,24},{20,28},{24,0},{28,4},{1,9},{5... | collective-permute-start | bytes 1572872 | tf_op jit(solution)/shard_map/cond/branch_1_fun/ppermute | solution.py:34
  394.7 1.1 copy-start.8
  395.8 24.5 %collective-permute-start.13 = (bf16[128,2048]{1,0:T(8,128)(2,1)}, bf16[128,2048]{1,0:T(8,128)(2,1)}, u32[]{:S(2)}, u32[]{:S(2)}) collective-permute-start(bf16[128,2048]{1,0:T(8,128)(2,1)} %get-tuple-element.157.refs_6_), channel_id=1, source_target_pairs={{0,8},{4,12},{8,16},{12,20},{16,24},{20,28},{24,0},{28,4},{1,9},{5... | collective-permute-start | bytes 1572872 | tf_op jit(solution)/shard_map/cond/branch_1_fun/ppermute | solution.py:34
  396.6 1.4 copy-start.3
  398.0 1.4 copy-start.9
  399.5 1.0 copy-start.27
  400.5 1.0 copy-start.33
  401.5 4.9 %copy-start.15 = (bf16[128,2048]{1,0:T(8,128)(2,1)S(1)}, bf16[128,2048]{1,0:T(8,128)(2,1)}, u32[]{:S(2)}) copy-start(bf16[128,2048]{1,0:T(8,128)(2,1)} %copy-done.14) | copy-start | bytes 1572868 | tf_op jit(solution)/shard_map/cond
  401.5 4.9 %copy-start.21 = (bf16[128,2048]{1,0:T(8,128)(2,1)S(1)}, bf16[128,2048]{1,0:T(8,128)(2,1)}, u32[]{:S(2)}) copy-start(bf16[128,2048]{1,0:T(8,128)(2,1)} %copy-done.20) | copy-start | bytes 1572868 | tf_op jit(solution)/shard_map/cond
  425.6 2.8 copy-start.58
  425.6 3.1 copy-start.61
  442.6 2.7 copy-start.72
  442.6 4.8 %copy-start.73 = (bf16[4,2048,384]{2,1,0:T(8,128)(2,1)}, bf16[4,2048,384]{2,1,0:T(8,128)(2,1)S(1)}, u32[]{:S(2)}) copy-start(bf16[4,2048,384]{2,1,0:T(8,128)(2,1)S(1)} %get-tuple-element.236) | copy-start | bytes 18874372
  442.6 5.3 %copy-start.74 = (bf16[4,128,2048]{2,1,0:T(8,128)(2,1)}, bf16[4,128,2048]{2,1,0:T(8,128)(2,1)S(1)}, u32[]{:S(2)}) copy-start(bf16[4,128,2048]{2,1,0:T(8,128)(2,1)S(1)} %get-tuple-element.237) | copy-start | bytes 6291460
  442.6 5.9 %copy-start.75 = (bf16[4,128,2048]{2,1,0:T(8,128)(2,1)}, bf16[4,128,2048]{2,1,0:T(8,128)(2,1)S(1)}, u32[]{:S(2)}) copy-start(bf16[4,128,2048]{2,1,0:T(8,128)(2,1)S(1)} %get-tuple-element.235) | copy-start | bytes 6291460
Sparse Core Ops, SparseCore 0:
  16.4 60.9 all-gather.15
  79.5 58.2 all-gather.13
where the time goes:
time: 462 us; the launch traced here: 456 us
  Pallas kernels  213 us (46%)
  waiting for transfers between devices  167 us (36%)
  local copies, waits for them, and re-layouts  23.3 us (5%)
  loops' own time  16.4 us (4%)
  between operations  15.2 us (3%)
  starting transfers between devices  12.9 us (3%)
  other arithmetic  8.59 us (2%)
    pallas_call x4, Pallas kernels, attention(): pl.pallas_call(partial(attention_kernel, 1.0 / math.sqrt(head_dim), 1.0 /...  111 us
    ppermute x10, waiting for transfers between devices, shifted(): lax.ppermute(value, 'gossip', [(i, (i + by) % size) for i in range(size)])  70.2 us
    all_gather x1, waiting for transfers between devices, update(): rows = lax.all_gather(out_grad, 'fsdp', axis=0, tiled=True)  48.5 us
    all_gather x1, waiting for transfers between devices, update(): normed = lax.all_gather(normed, 'fsdp', axis=0, tiled=True)  47.3 us
    pallas_call x4, Pallas kernels, momenta(): pl.pallas_call(partial(momenta_kernel, scale), grid=(width // block,), in...  45.1 us
    pallas_call x1, Pallas kernels, project(): pl.pallas_call(partial(project_kernel, 1.0 / math.sqrt(width)), grid=(seq...  23.4 us
    pallas_call x4, Pallas kernels, average(): pl.pallas_call(average_kernel, grid=(steps,), in_specs=in_specs, out_spec...  20.8 us
    cond x58, local copies, waits for them, and re-layouts  17.4 us
  transfers between devices with their start and end apart: 12, of which 5 were waited for; matrix products, arithmetic and copies ran while one was open for 2% of the time, Pallas kernels for 45%

commit v1 on v0

v1 whole, which is shorter than its diff:
```python
from functools import partial
import math

import jax
import jax.numpy as jnp
from jax import lax
from jax.experimental import pallas as pl
from jax.experimental.pallas import tpu as pltpu
from jax.sharding import PartitionSpec as P

HEADS = 16
LEVELS = 3

BETA = 0.9
RATE = 0.1
EPSILON = 1e-05

VMEM_LIMIT = 63 * 1024 * 1024
BLOCK = 512

SHORT = pl.CostEstimate(flops=1, bytes_accessed=1, transcendentals=0)


def product(left, right, left_dim=1, right_dim=0):
    return lax.dot_general(
        left, right, (((left_dim,), (right_dim,)), ((), ())), preferred_element_type=jnp.float32
    )


def params():
    return pltpu.CompilerParams(vmem_limit_bytes=VMEM_LIMIT)


def shifted(value, by):
    size = lax.axis_size("gossip")
    return lax.ppermute(value, "gossip", [(i, (i + by) % size) for i in range(size)])


def rotary_tables(seq_len, head_dim):
    half = head_dim // 2
    frequency = jnp.exp(
        -math.log(10000.0) * 2.0 * jnp.arange(half, dtype=jnp.float32) / head_dim
    )
    angles = jnp.arange(seq_len).astype(jnp.float32)[:, None] * frequency[None, :]
    return jnp.cos(angles), jnp.sin(angles)


def project_kernel(scale, rows_ref, weight_ref, cos_ref, sin_ref, q_ref, k_ref, v_ref):
    cosine, sine = cos_ref[...], sin_ref[...]
    width = cosine.shape[-1]
    projected = product(rows_ref[...], weight_ref[0]) * scale
    for which, out_ref in enumerate((q_ref, k_ref)):
        part = projected[:, which * width : (which + 1) * width]
        turned = part * cosine + pltpu.roll(part, width // 2, 1) * sine
        out_ref[...] = turned.astype(jnp.bfloat16)
    v_ref[...] = projected[:, 2 * width :].astype(jnp.bfloat16)


def project(head, rows, weights, cosine, sine):
    seq_len, width = rows.shape
    three = weights.shape[-1]
    head_dim = three // 3
    block = min(BLOCK, seq_len)
    out = jax.ShapeDtypeStruct((seq_len, head_dim), jnp.bfloat16)
    out_spec = pl.BlockSpec((block, head_dim), lambda i: (i, 0))
    return pl.pallas_call(
        partial(project_kernel, 1.0 / math.sqrt(width)),
        grid=(seq_len // block,),
        in_specs=[
            pl.BlockSpec((block, width), lambda i: (i, 0)),
            pl.BlockSpec((1, width, three), lambda i: (head, 0, 0)),
            out_spec,
            out_spec,
        ],
        out_specs=[out_spec] * 3,
        out_shape=[out] * 3,
        compiler_params=params(),
        cost_estimate=SHORT,
        name="project",
    )(rows, weights, cosine, sine)


def cotangent_kernel(scale, rows_ref, weight_ref, out_ref):
    rows = rows_ref[...]
    for head in range(weight_ref.shape[0]):
        out_ref[head] = (product(rows, weight_ref[head], 1, 1) * scale).astype(jnp.bfloat16)


def cotangent(rows, weights, scale):
    seq_len, width = rows.shape
    heads, head_dim, _ = weights.shape
    block = min(BLOCK, seq_len)
    return pl.pallas_call(
        partial(cotangent_kernel, scale),
        grid=(seq_len // block,),
        in_specs=[
            pl.BlockSpec((block, width), lambda i: (i, 0)),
            pl.BlockSpec((heads, head_dim, width), lambda i: (0, 0, 0)),
        ],
        out_specs=pl.BlockSpec((heads, block, head_dim), lambda i: (0, i, 0)),
        out_shape=jax.ShapeDtypeStruct((heads, seq_len, head_dim), jnp.bfloat16),
        compiler_params=params(),
        cost_estimate=SHORT,
        name="cotangent",
    )(rows, weights)


def folded(values, combine):
    rows, columns = values.shape
    return combine(values.reshape(rows // 8, 8, columns), 0)


def attention_kernel(
    scale,
    proj_scale,
    q_ref,
    k_ref,
    v_ref,
    g_ref,
    cos_ref,
    sin_ref,
    grad_ref,
    att_ref,
    s_ref,
    p_ref,
    d_ref,
    kt_ref,
    vt_ref,
    gk_ref,
    gv_ref,
):
    step = pl.program_id(0)
    block = s_ref.shape[1]
    head_dim = q_ref.shape[-1]
    half = head_dim // 2

    here = pl.ds(pl.multiple_of(step * block, block), block)
    queries = q_ref[here, :]
    grads = g_ref[0, here, :]
    kt_ref[step] = k_ref[here, :].T
    vt_ref[step] = v_ref[here, :].T
    gk_ref[step] = jnp.zeros(gk_ref.shape[1:], jnp.float32)
    gv_ref[step] = jnp.zeros(gv_ref.shape[1:], jnp.float32)

    def rows(tile):
        return pl.ds(pl.multiple_of(tile * block, block), block)

    scores = product(k_ref[here, :], queries, 1, 1)
    key_pos = lax.broadcasted_iota(jnp.int32, scores.shape, 0)
    query_pos = lax.broadcasted_iota(jnp.int32, scores.shape, 1)
    scores = jnp.where(key_pos <= query_pos, scores, -jnp.inf)
    s_ref[step] = scores

    def score(tile, top):
        scores = product(k_ref[rows(tile), :], queries, 1, 1)
        s_ref[tile] = scores
        return jnp.maximum(top, folded(scores, jnp.max))

    top = lax.fori_loop(0, step, score, folded(scores, jnp.max))
    factor = scale * math.log2(math.e)
    top = jnp.max(top, 0, keepdims=True) * factor

    def weigh(tile, sums):
        total, inner = sums
        weights = jnp.exp2(s_ref[tile] * factor - top)
        grad_probs = product(v_ref[rows(tile), :], grads, 1, 1)
        p_ref[tile] = weights
        d_ref[tile] = grad_probs
        return total + folded(weights, jnp.sum), inner + folded(weights * grad_probs, jnp.sum)

    zeros = jnp.zeros((8, block), jnp.float32)
    total, inner = lax.fori_loop(0, step + 1, weigh, (zeros, zeros))
    inverse = 1.0 / jnp.sum(total, 0, keepdims=True)
    inner = jnp.sum(inner, 0, keepdims=True) * inverse

    def back(tile, sums):
        att, grad_q = sums
        probs = p_ref[tile] * inverse
        probs_b = probs.astype(jnp.bfloat16)
        grad_scores = (probs * (d_ref[tile] - inner)).astype(jnp.bfloat16)
        gv_ref[tile] += product(probs_b, grads)
        gk_ref[tile] += product(grad_scores, queries)
        return att + product(vt_ref[tile], probs_b), grad_q + product(kt_ref[tile], grad_scores)

    zeros = jnp.zeros((head_dim, block), jnp.float32)
    att, grad_q = lax.fori_loop(0, step + 1, back, (zeros, zeros))

    def unrotate(grad, where):
        cosine, sine = cos_ref[:, where], sin_ref[:, where]
        first, second = grad[:half], grad[half:]
        factor = scale * proj_scale
        return (
            ((first * cosine + second * sine) * factor).astype(jnp.bfloat16),
            ((second * cosine - first * sine) * factor).astype(jnp.bfloat16),
        )

    att_ref[:, here] = att.astype(jnp.bfloat16)
    first, second = unrotate(grad_q, here)
    grad_ref[:half, here] = first
    grad_ref[half:head_dim, here] = second

    @pl.when(step == pl.num_programs(0) - 1)
    def finish():
        def keys(tile, carry):
            where = rows(tile)
            first, second = unrotate(gk_ref[tile].T, where)
            grad_ref[head_dim : head_dim + half, where] = first
            grad_ref[head_dim + half : 2 * head_dim, where] = second
            values = gv_ref[tile].T * proj_scale
            grad_ref[2 * head_dim :, where] = values.astype(jnp.bfloat16)
            return carry

        lax.fori_loop(0, pl.num_programs(0), keys, 0)


def attention(head, queries, keys, values, grads, cosine_t, sine_t, width):
    seq_len, head_dim = queries.shape
    block = min(BLOCK, seq_len)
    tiles = seq_len // block
    of_head = pl.BlockSpec((seq_len, head_dim), lambda i: (0, 0))
    stacked = pl.BlockSpec((1, seq_len, head_dim), lambda i: (head, 0, 0))
    whole = pl.BlockSpec((head_dim // 2, seq_len), lambda i: (0, 0))
    return pl.pallas_call(
        partial(attention_kernel, 1.0 / math.sqrt(head_dim), 1.0 / math.sqrt(width)),
        grid=(tiles,),
        in_specs=[of_head] * 3 + [stacked] + [whole] * 2,
        out_specs=[
            pl.BlockSpec((3 * head_dim, seq_len), lambda i: (0, 0)),
            pl.BlockSpec((head_dim, seq_len), lambda i: (0, 0)),
        ],
        out_shape=[
            jax.ShapeDtypeStruct((3 * head_dim, seq_len), jnp.bfloat16),
            jax.ShapeDtypeStruct((head_dim, seq_len), jnp.bfloat16),
        ],
        scratch_shapes=[pltpu.VMEM((tiles, block, block), jnp.float32)] * 3
        + [pltpu.VMEM((tiles, head_dim, block), jnp.bfloat16)] * 2
        + [pltpu.VMEM((tiles, block, head_dim), jnp.float32)] * 2,
        compiler_params=params(),
        cost_estimate=SHORT,
        name="attention",
    )(queries, keys, values, grads, cosine_t, sine_t)


def momenta_kernel(
    scale, grad_ref, att_ref, normed_ref, rows_ref, mqkv_ref, mout_ref, moved_ref
):
    three = grad_ref.shape[0]
    grad = product(grad_ref[...], normed_ref[...]).T.astype(jnp.bfloat16)
    moved = BETA * mqkv_ref[0].astype(jnp.float32) + grad.astype(jnp.float32)
    moved_ref[:, :three] = moved.astype(jnp.bfloat16)
    grad = (product(att_ref[...], rows_ref[...]) * scale).astype(jnp.bfloat16)
    moved = BETA * mout_ref[0].astype(jnp.float32) + grad.astype(jnp.float32)
    moved_ref[:, three:] = moved.T.astype(jnp.bfloat16)


def momenta(head, piece, grad_proj, attended, normed, rows, mom_qkv, mom_out, scale):
    first, count, block = piece
    seq_len = normed.shape[0]
    three, head_dim = grad_proj.shape[0], attended.shape[0]
    return pl.pallas_call(
        partial(momenta_kernel, scale),
        grid=(count,),
        in_specs=[
            pl.BlockSpec((three, seq_len), lambda i: (0, 0)),
            pl.BlockSpec((head_dim, seq_len), lambda i: (0, 0)),
            pl.BlockSpec((seq_len, block), lambda i: (0, first + i)),
            pl.BlockSpec((seq_len, block), lambda i: (0, first + i)),
            pl.BlockSpec((1, block, three), lambda i: (head, first + i, 0)),
            pl.BlockSpec((1, head_dim, block), lambda i: (head, 0, first + i)),
        ],
        out_specs=pl.BlockSpec((block, three + head_dim), lambda i: (i, 0)),
        out_shape=jax.ShapeDtypeStruct((count * block, three + head_dim), jnp.bfloat16),
        compiler_params=params(),
        cost_estimate=SHORT,
        name="momenta",
    )(grad_proj, attended, normed, rows, mom_qkv, mom_out)


def average_kernel(rate_ref, qkv, other_qkv, out, other_out, moment, other_moment, *refs):
    rate = rate_ref[0, 0]
    new_qkv, new_out, new_mom_qkv, new_mom_out = refs[-4:]
    three = qkv.shape[-1]

    def halfway(own, other):
        return ((own.astype(jnp.float32) + other.astype(jnp.float32)) * 0.5).astype(jnp.bfloat16)

    def moved(weight, moment):
        new = weight.astype(jnp.float32) - rate * moment.astype(jnp.float32)
        return new.astype(jnp.bfloat16)

    own, other = moment[:, :three], other_moment[:, :three]
    new_qkv[0] = halfway(moved(qkv[0], own), moved(other_qkv[0], other))
    new_mom_qkv[0] = halfway(own, other)
    own = moment[:, three:].astype(jnp.float32).T
    other = other_moment[:, three:].astype(jnp.float32).T
    new_out[0] = halfway(moved(out[0], own), moved(other_out[0], other))
    new_mom_out[0] = halfway(own, other)


def average(head, piece, rate, own, other, moment, other_moment, previous):
    first, count, block = piece
    (qkv, out), (other_qkv, other_out) = own, other
    three, head_dim = qkv.shape[-1], out.shape[1]
    high = pl.BlockSpec((1, block, three), lambda i: (head, first + i, 0))
    wide = pl.BlockSpec((1, head_dim, block), lambda i: (head, 0, first + i))
    packed = pl.BlockSpec((block, three + head_dim), lambda i: (i, 0))
    in_specs = [pl.BlockSpec(memory_space=pltpu.SMEM), high, high, wide, wide, packed, packed]
    args = [rate, qkv, other_qkv, out, other_out, moment, other_moment]
    aliases = {}
    if previous is not None:
        aliases = {len(args) + i: i for i in range(4)}
        args += list(previous)
        in_specs += [pl.BlockSpec(memory_space=pl.ANY)] * 4
    return pl.pallas_call(
        average_kernel,
        grid=(count,),
        in_specs=in_specs,
        out_specs=[high, wide] * 2,
        out_shape=[jax.ShapeDtypeStruct(w.shape, jnp.bfloat16) for w in own] * 2,
        input_output_aliases=aliases,
        compiler_params=params(),
        cost_estimate=SHORT,
        name="average",
    )(*args)


def pieces_of(head, heads, width):
    block = min(BLOCK, width)
    blocks = width // block
    if head < heads - 1 or blocks < 4:
        return [(0, blocks, block)]
    return [(0, blocks - 2, block), (blocks - 2, 1, block), (blocks - 1, 1, block)]


def update(by, inputs, out_grad, norm_gain, w_qkv, w_out, mom_qkv, mom_out, rate):
    own = (w_qkv, w_out)
    other = tuple(shifted(w, by) for w in own)

    rows_f = inputs.astype(jnp.float32)
    stats = lax.rsqrt(jnp.mean(rows_f * rows_f, -1, keepdims=True) + EPSILON)
    normed = (rows_f * stats * norm_gain[None, :]).astype(jnp.bfloat16)
    normed = lax.all_gather(normed, "fsdp", axis=0, tiled=True)
    rows = lax.all_gather(out_grad, "fsdp", axis=0, tiled=True)

    seq_len, width = normed.shape
    heads, head_dim, _ = w_out.shape
    out_scale = 1.0 / math.sqrt(HEADS * head_dim)
    cosine, sine = rotary_tables(seq_len, head_dim)
    full_cosine = jnp.concatenate([cosine, cosine], -1)
    full_sine = jnp.concatenate([-sine, sine], -1)
    grads = cotangent(rows, w_out, out_scale)
    made = []
    for head in range(heads):
        queries, keys, values = project(head, normed, w_qkv, full_cosine, full_sine)
        grad_proj, attended = attention(
            head, queries, keys, values, grads, cosine.T, sine.T, width
        )
        for piece in pieces_of(head, heads, width):
            moment = momenta(
                head, piece, grad_proj, attended, normed, rows, mom_qkv, mom_out, out_scale
            )
            normed, moment = lax.optimization_barrier((normed, moment))
            made.append((head, piece, moment, shifted(moment, by)))
    results = None
    for head, piece, moment, other_moment in made:
        results = average(head, piece, rate, own, other, moment, other_moment, results)
    return tuple(results)


def per_device(inputs, out_grad, norm_gain, w_qkv, w_out, mom_qkv, mom_out, step_index):
    rate = RATE * (step_index[0].astype(jnp.float32) + 1.0) / (4.0 * LEVELS)
    exponent = jnp.remainder(step_index[0], LEVELS)
    results = lax.switch(
        exponent,
        [partial(update, 1 << level) for level in range(LEVELS)],
        inputs[0],
        out_grad[0],
        norm_gain[0],
        w_qkv[0],
        w_out[0],
        mom_qkv[0],
        mom_out[0],
        rate.reshape(1, 1),
    )
    return tuple(r[None] for r in results)


def solution(mesh):
    return jax.shard_map(
        per_device,
        mesh=mesh,
        in_specs=(
            P("gossip", "fsdp", None),
            P("gossip", "fsdp", None),
            P("gossip", None),
            P("gossip", "fsdp", None, None),
            P("gossip", "fsdp", None, None),
            P("gossip", "fsdp", None, None),
            P("gossip", "fsdp", None, None),
            P(),
        ),
        out_specs=(
            P("gossip", "fsdp", None, None),
            P("gossip", "fsdp", None, None),
            P("gossip", "fsdp", None, None),
            P("gossip", "fsdp", None, None),
        ),
        check_vma=False,
    )
```

time: 462 us -> 792 us (1.71)
  waiting for transfers between devices: 167 us -> 500 us
    ppermute x10 -> x8, waiting for transfers between devices: 70.2 us -> 405 us  [shifted(): lax.ppermute(value, 'gossip', [(i, (i + by) % size) for i in range(size)])]
    pallas_call x4, Pallas kernels: 111 us -> 71.8 us  [attention(): pl.pallas_call(partial(attention_kernel, 1.0 / math.sqrt(head_dim), 1.0 /...]
    pallas_call x8 -> x12, Pallas kernels: 65.9 us -> 85.7 us  [the longest x6 53.4 us: momenta(): pl.pallas_call(partial(momenta_kernel, scale), grid=(count,), in_specs=[p...]
    pallas_call x1 -> x4, Pallas kernels: 23.4 us -> 36 us  [project(): pl.pallas_call(partial(project_kernel, 1.0 / math.sqrt(width)), grid=(seq...]
    cond x58 -> x12, local copies, waits for them, and re-layouts: 17.4 us -> 9.61 us
  transfers between devices with their start and end apart: 12 -> 10, of which waited for: 5 -> 9; matrix products, arithmetic and copies ran while one was open for 2% -> 1% of each run, Pallas kernels for 45% -> 26%
where the time goes in v1:
time: 792 us; the launch traced here: 783 us
  waiting for transfers between devices  500 us (63%)
  Pallas kernels  206 us (26%)
  loops' own time  22.6 us (3%)
  local copies, waits for them, and re-layouts  15.5 us (2%)
  between operations  15.3 us (2%)
  starting transfers between devices  12.5 us (2%)
  other arithmetic  11 us (1%)
    ppermute x8, waiting for transfers between devices, shifted(): lax.ppermute(value, 'gossip', [(i, (i + by) % size) for i in range(size)])  405 us
    pallas_call x4, Pallas kernels, attention(): pl.pallas_call(partial(attention_kernel, 1.0 / math.sqrt(head_dim), 1.0 /...  71.8 us
    pallas_call x6, Pallas kernels, momenta(): pl.pallas_call(partial(momenta_kernel, scale), grid=(count,), in_specs=[p...  53.4 us
    all_gather x1, waiting for transfers between devices, update(): normed = lax.all_gather(normed, 'fsdp', axis=0, tiled=True)  48.1 us
    all_gather x1, waiting for transfers between devices, update(): rows = lax.all_gather(out_grad, 'fsdp', axis=0, tiled=True)  46.6 us
    pallas_call x4, Pallas kernels, project(): pl.pallas_call(partial(project_kernel, 1.0 / math.sqrt(width)), grid=(seq...  36 us
    pallas_call x6, Pallas kernels, average(): pl.pallas_call(average_kernel, grid=(count,), in_specs=in_specs, out_spec...  32.3 us
    another operation x1, loops' own time, per_device(): lax.switch(exponent, [partial(update, 1 << level) for level in range(LEVE...  22.6 us
  transfers between devices with their start and end apart: 10, of which 9 were waited for; matrix products, arithmetic and copies ran while one was open for 1% of the time, Pallas kernels for 26%

profile of v1, /device:TPU:0, one launch (start us, length us, event | category | flops | bytes accessed | tf_op | source)
XLA Modules:
  0.0 783.1 jit_solution(10306142380873858541)
XLA Ops:
  7.8 762.0 %conditional.1 = ((bf16[4,2048,384]{2,1,0:T(8,128)(2,1)}, bf16[4,128,2048]{2,1,0:T(8,128)(2,1)}, bf16[4,2048,384]{2,1,0:T(8,128)(2,1)}, bf16[4,128,2048]{2,1,0:T...) conditional(s32[]{:T(128)} %clamp.3, (s32[]{:T(128)}, ...), branch_computations={%region_0.2_spmd, %region_2.4_spmd, %region_4.6_spmd} | conditional | flops 8260184 | bytes 195110224 | solution.py:373
  29.4 0.0 copy-start.5
  29.4 0.0 all-gather.20.cloned.1.call-start
  29.4 0.0 copy-start.15
  29.5 0.7 all-gather.20.cloned.1.call-update
  30.1 0.0 all-gather.18.cloned.1.call-start
  30.2 0.8 copy-done.5
  31.0 0.5 fusion.8
  31.5 1.9 fusion.10
  33.3 0.0 all-gather.18.cloned.1.call-update
  33.4 4.1 collective-permute-start.16
  37.5 0.1 collective-permute-start.17
  37.6 3.7 fusion.11
  41.3 1.9 pad_maximum_fusion.4
  43.2 3.0 multiply_sine_fusion.5
  46.2 46.6 %all-gather.20.cloned.1.call-done = bf16[1,2048,2048]{2,1,0:T(8,128)(2,1)} async-done(((bf16[1,512,2048]{2,1,0:T(8,128)(2,1)}), bf16[1,2048,2048]{2,1,0:T(8,128)(2,1)}) %all-gather.20.cloned.1.call-update) | async-done | bytes 8388624 | tf_op jit(solution)/shard_map/cond/branch_2_fun/all_gather | solution.py:343
  92.8 12.4 %cotangent.5.g_ref = bf16[4,2048,128]{2,1,0:T(8,128)(2,1)} custom-call(bf16[2048,2048]{1,0:T(8,128)(2,1)} %bitcast.122, bf16[4,128,2048]{2,1,0:T(8,128)(2,1)} %bitcast.20.weight_ref.out), custom_call_target="tpu_custom_call" | custom-call | flops 1 | bytes 1 | tf_op jit(solution)/shard_map/cond/branch_2_fun/cotangent/pallas_call | solution.py:93
  105.2 48.1 %all-gather.18.cloned.1.call-done.rows_ref.normed_ref = bf16[2048,2048]{1,0:T(8,128)(2,1)} async-done(((bf16[512,2048]{1,0:T(8,128)(2,1)}), bf16[2048,2048]{1,0:T(8,128)(2,1)}) %all-gather.18.cloned.1.call-update) | async-done | bytes 8388624 | tf_op jit(solution)/shard_map/cond/branch_2_fun/all_gather | solution.py:342
  153.3 9.0 %project.20 = (bf16[2048,128]{1,0:T(8,128)(2,1)}, bf16[2048,128]{1,0:T(8,128)(2,1)}, bf16[2048,128]{1,0:T(8,128)(2,1)}) custom-call(bf16[2048,2048]{1,0:T(8,128)(2,1)} %all-gather.18.cloned.1.call-done.rows_ref.normed_ref, bf16[4,2048,384]{2,1,0:T(8,128)(2,1)} %bitcast.62, f32[2048,128]{1,0:T(8,128)} %get-tuple-element.318.cos_ref, ...), custom_call_target="tpu_custom_call" | custom-call | flops 1 | bytes 1 | tf_op jit(solution)/shard_map/cond/branch_2_fun/project/pallas_call | solution.py:66
  162.3 18.0 %attention.20 = (bf16[384,2048]{1,0:T(8,128)(2,1)}, bf16[128,2048]{1,0:T(8,128)(2,1)}) custom-call(bf16[2048,128]{1,0:T(8,128)(2,1)} %get-tuple-element.231.q_ref, bf16[2048,128]{1,0:T(8,128)(2,1)} %get-tuple-element.232.k_ref, bf16[2048,128]{1,0:T(8,128)(2,1)} %get-tuple-element.233.v_ref, bf16[4,2048,128]{2,1,0:T(8,128)(2,1)} %cotangent.5.g_ref, ...), custom_call_target="tpu_custom_call" | custom-call | flops 1 | bytes 1 | tf_op jit(solution)/shard_map/cond/branch_2_fun/attention/pallas_call | solution.py:223
  180.2 11.9 %momenta.30.moment = bf16[2048,512]{1,0:T(8,128)(2,1)} custom-call(bf16[384,2048]{1,0:T(8,128)(2,1)} %get-tuple-element.235.grad_ref, bf16[128,2048]{1,0:T(8,128)(2,1)} %get-tuple-element.236.att_ref, bf16[2048,2048]{1,0:T(8,128)(2,1)} %all-gather.18.cloned.1.call-done.rows_ref.normed_ref, bf16[2048,2048]{1,0:T(8,128)(2,1)} %bitcast.123, ...), custom_call_target="tpu_custom_call" | custom-call | flops 1 | bytes 1 | tf_op jit(solution)/shard_map/cond/branch_2_fun/momenta/pallas_call | solution.py:260
  192.1 2.4 collective-permute-start.23
  194.5 9.0 %project.21 = (bf16[2048,128]{1,0:T(8,128)(2,1)}, bf16[2048,128]{1,0:T(8,128)(2,1)}, bf16[2048,128]{1,0:T(8,128)(2,1)}) custom-call(bf16[2048,2048]{1,0:T(8,128)(2,1)} %all-gather.18.cloned.1.call-done.rows_ref.normed_ref, bf16[4,2048,384]{2,1,0:T(8,128)(2,1)} %bitcast.63, f32[2048,128]{1,0:T(8,128)} %get-tuple-element.318.cos_ref, ...), custom_call_target="tpu_custom_call" | custom-call | flops 1 | bytes 1 | tf_op jit(solution)/shard_map/cond/branch_2_fun/project/pallas_call | solution.py:66
  203.5 17.9 %attention.21 = (bf16[384,2048]{1,0:T(8,128)(2,1)}, bf16[128,2048]{1,0:T(8,128)(2,1)}) custom-call(bf16[2048,128]{1,0:T(8,128)(2,1)} %get-tuple-element.240.q_ref, bf16[2048,128]{1,0:T(8,128)(2,1)} %get-tuple-element.241.k_ref, bf16[2048,128]{1,0:T(8,128)(2,1)} %get-tuple-element.242.v_ref, bf16[4,2048,128]{2,1,0:T(8,128)(2,1)} %cotangent.5.g_ref, ...), custom_call_target="tpu_custom_call" | custom-call | flops 1 | bytes 1 | tf_op jit(solution)/shard_map/cond/branch_2_fun/attention/pallas_call | solution.py:223
  221.4 11.9 %momenta.31.moment = bf16[2048,512]{1,0:T(8,128)(2,1)} custom-call(bf16[384,2048]{1,0:T(8,128)(2,1)} %get-tuple-element.243.grad_ref, bf16[128,2048]{1,0:T(8,128)(2,1)} %get-tuple-element.244.att_ref, bf16[2048,2048]{1,0:T(8,128)(2,1)} %all-gather.18.cloned.1.call-done.rows_ref.normed_ref, bf16[2048,2048]{1,0:T(8,128)(2,1)} %bitcast.124, ...), custom_call_target="tpu_custom_call" | custom-call | flops 1 | bytes 1 | tf_op jit(solution)/shard_map/cond/branch_2_fun/momenta/pallas_call | solution.py:260
  233.2 9.0 %project.22 = (bf16[2048,128]{1,0:T(8,128)(2,1)}, bf16[2048,128]{1,0:T(8,128)(2,1)}, bf16[2048,128]{1,0:T(8,128)(2,1)}) custom-call(bf16[2048,2048]{1,0:T(8,128)(2,1)} %all-gather.18.cloned.1.call-done.rows_ref.normed_ref, bf16[4,2048,384]{2,1,0:T(8,128)(2,1)} %bitcast.64, f32[2048,128]{1,0:T(8,128)} %get-tuple-element.318.cos_ref, ...), custom_call_target="tpu_custom_call" | custom-call | flops 1 | bytes 1 | tf_op jit(solution)/shard_map/cond/branch_2_fun/project/pallas_call | solution.py:66
  242.2 0.5 collective-permute-start.22
  242.8 18.1 %attention.22 = (bf16[384,2048]{1,0:T(8,128)(2,1)}, bf16[128,2048]{1,0:T(8,128)(2,1)}) custom-call(bf16[2048,128]{1,0:T(8,128)(2,1)} %get-tuple-element.246.q_ref, bf16[2048,128]{1,0:T(8,128)(2,1)} %get-tuple-element.247.k_ref, bf16[2048,128]{1,0:T(8,128)(2,1)} %get-tuple-element.248.v_ref, bf16[4,2048,128]{2,1,0:T(8,128)(2,1)} %cotangent.5.g_ref, ...), custom_call_target="tpu_custom_call" | custom-call | flops 1 | bytes 1 | tf_op jit(solution)/shard_map/cond/branch_2_fun/attention/pallas_call | solution.py:223
  260.9 11.9 %momenta.32.moment = bf16[2048,512]{1,0:T(8,128)(2,1)} custom-call(bf16[384,2048]{1,0:T(8,128)(2,1)} %get-tuple-element.249.grad_ref, bf16[128,2048]{1,0:T(8,128)(2,1)} %get-tuple-element.250.att_ref, bf16[2048,2048]{1,0:T(8,128)(2,1)} %all-gather.18.cloned.1.call-done.rows_ref.normed_ref, bf16[2048,2048]{1,0:T(8,128)(2,1)} %bitcast.125, ...), custom_call_target="tpu_custom_call" | custom-call | flops 1 | bytes 1 | tf_op jit(solution)/shard_map/cond/branch_2_fun/momenta/pallas_call | solution.py:260
  272.8 2.4 collective-permute-start.21
  275.2 9.0 %project.23 = (bf16[2048,128]{1,0:T(8,128)(2,1)}, bf16[2048,128]{1,0:T(8,128)(2,1)}, bf16[2048,128]{1,0:T(8,128)(2,1)}) custom-call(bf16[2048,2048]{1,0:T(8,128)(2,1)} %all-gather.18.cloned.1.call-done.rows_ref.normed_ref, bf16[4,2048,384]{2,1,0:T(8,128)(2,1)} %bitcast.65, f32[2048,128]{1,0:T(8,128)} %get-tuple-element.318.cos_ref, ...), custom_call_target="tpu_custom_call" | custom-call | flops 1 | bytes 1 | tf_op jit(solution)/shard_map/cond/branch_2_fun/project/pallas_call | solution.py:66
  284.2 17.9 %attention.23 = (bf16[384,2048]{1,0:T(8,128)(2,1)}, bf16[128,2048]{1,0:T(8,128)(2,1)}) custom-call(bf16[2048,128]{1,0:T(8,128)(2,1)} %get-tuple-element.252.q_ref, bf16[2048,128]{1,0:T(8,128)(2,1)} %get-tuple-element.253.k_ref, bf16[2048,128]{1,0:T(8,128)(2,1)} %get-tuple-element.254.v_ref, bf16[4,2048,128]{2,1,0:T(8,128)(2,1)} %cotangent.5.g_ref, ...), custom_call_target="tpu_custom_call" | custom-call | flops 1 | bytes 1 | tf_op jit(solution)/shard_map/cond/branch_2_fun/attention/pallas_call | solution.py:223
  302.1 7.7 momenta.33.moment
  309.8 223.9 %collective-permute-done.17.other_out = bf16[4,128,2048]{2,1,0:T(8,128)(2,1)} collective-permute-done((bf16[4,128,2048]{2,1,0:T(8,128)(2,1)}, bf16[4,128,2048]{2,1,0:T(8,128)(2,1)}, u32[]{:S(2)}, u32[]{:S(2)}) %collective-permute-start.17) | collective-permute-done | bytes 2097184 | tf_op jit(solution)/shard_map/cond/branch_2_fun/ppermute | solution.py:36
  533.7 5.1 momenta.34.moment
  538.7 2.9 collective-permute-start.19
  541.6 5.0 momenta.35.moment
  546.7 65.6 %collective-permute-done.23.other_moment = bf16[2048,512]{1,0:T(8,128)(2,1)} collective-permute-done((bf16[2048,512]{1,0:T(8,128)(2,1)}, bf16[2048,512]{1,0:T(8,128)(2,1)}, u32[]{:S(2)}, u32[]{:S(2)}) %collective-permute-start.23) | collective-permute-done | bytes 2097184 | tf_op jit(solution)/shard_map/cond/branch_2_fun/ppermute | solution.py:36
  612.3 0.0 collective-permute-start.18
  613.0 7.1 average.30
  620.1 48.4 %collective-permute-done.22.other_moment = bf16[2048,512]{1,0:T(8,128)(2,1)} collective-permute-done((bf16[2048,512]{1,0:T(8,128)(2,1)}, bf16[2048,512]{1,0:T(8,128)(2,1)}, u32[]{:S(2)}, u32[]{:S(2)}) %collective-permute-start.22) | collective-permute-done | bytes 2097184 | tf_op jit(solution)/shard_map/cond/branch_2_fun/ppermute | solution.py:36
  668.5 7.1 average.31
  675.6 37.9 %collective-permute-done.21.other_moment = bf16[2048,512]{1,0:T(8,128)(2,1)} collective-permute-done((bf16[2048,512]{1,0:T(8,128)(2,1)}, bf16[2048,512]{1,0:T(8,128)(2,1)}, u32[]{:S(2)}, u32[]{:S(2)}) %collective-permute-start.21) | collective-permute-done | bytes 2097184 | tf_op jit(solution)/shard_map/cond/branch_2_fun/ppermute | solution.py:36
  713.4 7.1 average.32
  720.5 15.4 %collective-permute-done.20.other_moment = bf16[1024,512]{1,0:T(8,128)(2,1)} collective-permute-done((bf16[1024,512]{1,0:T(8,128)(2,1)}, bf16[1024,512]{1,0:T(8,128)(2,1)}, u32[]{:S(2)}, u32[]{:S(2)}) %collective-permute-start.20) | collective-permute-done | bytes 1048608 | tf_op jit(solution)/shard_map/cond/branch_2_fun/ppermute | solution.py:36
  735.9 4.6 average.33
  740.4 6.7 collective-permute-done.19.other_moment
  747.1 3.2 average.34
  750.4 7.1 collective-permute-done.18.other_moment
  757.4 0.8 copy-done.12
  758.2 3.2 average.35
  761.4 2.9 copy.177
  764.4 0.5 copy-done.2
  764.9 0.2 copy.178
  765.1 2.8 copy.179
  767.9 1.6 copy.180
  769.8 0.0 copy-start.6
  769.8 0.0 copy-start.7
  769.8 0.0 copy-start.8
  769.8 0.0 copy-start.9
  769.8 2.7 copy-done.6
  772.5 2.1 copy-done.7
  774.6 0.5 copy-done.8
  775.1 0.6 copy-done.9
  (8 shorter events, 0.0 us)
Async XLA Ops:
  29.4 1.6 copy-start.5
  29.4 63.4 %all-gather.20.cloned.1.call-start = ((), (), s32[]{:S(2)}) async-start(), calls=%async_computation.5 | async-start | bytes 10485760 | tf_op jit(solution)/shard_map/cond/branch_2_fun/all_gather | solution.py:343
  29.4 2.0 copy-start.15
  30.1 123.1 %all-gather.18.cloned.1.call-start = ((), (), s32[]{:S(2)}) async-start(), calls=%async_computation.4 | async-start | bytes 10485760 | tf_op jit(solution)/shard_map/cond/branch_2_fun/all_gather | solution.py:342
  33.4 505.4 %collective-permute-start.16 = (bf16[4,2048,384]{2,1,0:T(8,128)(2,1)}, bf16[4,2048,384]{2,1,0:T(8,128)(2,1)}, u32[]{:S(2)}, u32[]{:S(2)}) collective-permute-start(bf16[4,2048,384]{2,1,0:T(8,128)(2,1)} %bitcast.61), channel_id=1, source_target_pairs={{0,16},{4,20},{8,24},{12,28},{16,0},{20,4},{24,8},{28,12},{1,17},{... | collective-permute-start | bytes 18874376 | tf_op jit(solution)/shard_map/cond/branch_2_fun/ppermute | solution.py:36
  37.5 496.2 %collective-permute-start.17 = (bf16[4,128,2048]{2,1,0:T(8,128)(2,1)}, bf16[4,128,2048]{2,1,0:T(8,128)(2,1)}, u32[]{:S(2)}, u32[]{:S(2)}) collective-permute-start(bf16[4,128,2048]{2,1,0:T(8,128)(2,1)} %bitcast.20.weight_ref.out), channel_id=1, source_target_pairs={{0,16},{4,20},{8,24},{12,28},{16,0},{20,4},{24,8},{28,12},{1,17},{... | collective-permute-start | bytes 6291464 | tf_op jit(solution)/shard_map/cond/branch_2_fun/ppermute | solution.py:36
  192.1 420.2 %collective-permute-start.23 = (bf16[2048,512]{1,0:T(8,128)(2,1)}, bf16[2048,512]{1,0:T(8,128)(2,1)}, u32[]{:S(2)}, u32[]{:S(2)}) collective-permute-start(bf16[2048,512]{1,0:T(8,128)(2,1)} %momenta.30.moment), channel_id=1, source_target_pairs={{0,16},{4,20},{8,24},{12,28},{16,0},{20,4},{24,8},{28,12},{1,17},{... | collective-permute-start | bytes 6291464 | tf_op jit(solution)/shard_map/cond/branch_2_fun/ppermute | solution.py:36
  242.2 426.2 %collective-permute-start.22 = (bf16[2048,512]{1,0:T(8,128)(2,1)}, bf16[2048,512]{1,0:T(8,128)(2,1)}, u32[]{:S(2)}, u32[]{:S(2)}) collective-permute-start(bf16[2048,512]{1,0:T(8,128)(2,1)} %momenta.31.moment), channel_id=1, source_target_pairs={{0,16},{4,20},{8,24},{12,28},{16,0},{20,4},{24,8},{28,12},{1,17},{... | collective-permute-start | bytes 6291464 | tf_op jit(solution)/shard_map/cond/branch_2_fun/ppermute | solution.py:36
  272.8 440.7 %collective-permute-start.21 = (bf16[2048,512]{1,0:T(8,128)(2,1)}, bf16[2048,512]{1,0:T(8,128)(2,1)}, u32[]{:S(2)}, u32[]{:S(2)}) collective-permute-start(bf16[2048,512]{1,0:T(8,128)(2,1)} %momenta.32.moment), channel_id=1, source_target_pairs={{0,16},{4,20},{8,24},{12,28},{16,0},{20,4},{24,8},{28,12},{1,17},{... | collective-permute-start | bytes 6291464 | tf_op jit(solution)/shard_map/cond/branch_2_fun/ppermute | solution.py:36
  533.7 202.2 %collective-permute-start.20 = (bf16[1024,512]{1,0:T(8,128)(2,1)}, bf16[1024,512]{1,0:T(8,128)(2,1)}, u32[]{:S(2)}, u32[]{:S(2)}) collective-permute-start(bf16[1024,512]{1,0:T(8,128)(2,1)} %momenta.33.moment), channel_id=1, source_target_pairs={{0,16},{4,20},{8,24},{12,28},{16,0},{20,4},{24,8},{28,12},{1,17},{... | collective-permute-start | bytes 3145736 | tf_op jit(solution)/shard_map/cond/branch_2_fun/ppermute | solution.py:36
  538.7 208.4 %collective-permute-start.19 = (bf16[512,512]{1,0:T(8,128)(2,1)}, bf16[512,512]{1,0:T(8,128)(2,1)}, u32[]{:S(2)}, u32[]{:S(2)}) collective-permute-start(bf16[512,512]{1,0:T(8,128)(2,1)} %momenta.34.moment), channel_id=1, source_target_pairs={{0,16},{4,20},{8,24},{12,28},{16,0},{20,4},{24,8},{28,12},{1,17},{... | collective-permute-start | bytes 1572872 | tf_op jit(solution)/shard_map/cond/branch_2_fun/ppermute | solution.py:36
  612.3 145.1 %collective-permute-start.18 = (bf16[512,512]{1,0:T(8,128)(2,1)}, bf16[512,512]{1,0:T(8,128)(2,1)S(1)}, u32[]{:S(2)}, u32[]{:S(2)}) collective-permute-start(bf16[512,512]{1,0:T(8,128)(2,1)} %momenta.35.moment), channel_id=1, source_target_pairs={{0,16},{4,20},{8,24},{12,28},{16,0},{20,4},{24,8},{28,12},{1,17},{... | collective-permute-start | bytes 1572872 | tf_op jit(solution)/shard_map/cond/branch_2_fun/ppermute | solution.py:36
  757.4 0.8 copy-start.12
  761.4 3.4 copy-start.2
  769.8 2.7 copy-start.6
  769.8 4.8 copy-start.7
  769.8 5.3 copy-start.8
  769.8 5.9 copy-start.9
Sparse Core Ops, SparseCore 0:
  31.8 60.9 all-gather.19
  94.9 58.2 all-gather.17
